TPU v7x, 32 devices: a whole 2x2x4 slice. The times are simulated.
32 devices in a mesh: seq: 8 (over y, x, core), head: 4 (over z).
Axes of the slice: x: 2, y: 2, z: 4, core: 2. Of those that a mesh axis runs over, the one named last changes fastest.
Arguments:
- tokens: bfloat16 [16384, 2048], P(('seq', 'head')), may hold values from -6 to 6
- w_query: bfloat16 [2048, 2048], P(None, 'head'), may hold values from -0.125 to 0.125
- w_key: bfloat16 [2048, 2048], P(None, 'head'), may hold values from -0.125 to 0.125
- w_value: bfloat16 [2048, 2048], P(None, 'head'), may hold values from -0.125 to 0.125
- w_beta: bfloat16 [2048, 16], P(None, 'head'), may hold values from -0.125 to 0.125
- beta_gain: float32 [16], P('head'), may hold values from 0.0005 to 0.5
- norm_gain: float32 [2048], P('head'), may hold values from 0.1 to 1.9
- w_out: bfloat16 [2048, 2048], P('head'), may hold values from -0.125 to 0.125
Outputs:
- mixed: bfloat16 [16384, 2048], P(('seq', 'head'))
All inputs are finite; a program needn't handle non-finite values.
Results may differ from a plain program's by a relative error of at most 0.0085.
Values may be sent and summed in bfloat16 or wider, within the bound.
A program may use at most 192 MiB of HBM per device.

v0:
```python
import jax
import jax.numpy as jnp
from jax import lax
from jax.sharding import PartitionSpec as P

SPAN = 64
highest = lax.Precision.HIGHEST


def entering(part, axis, combine, identity):
    place = lax.axis_index(axis)
    gathered = jax.tree.map(lambda a: lax.all_gather(a, axis), part)
    state = jax.tree.map(lambda a, e: jnp.zeros_like(a) + jnp.asarray(e, a.dtype), part, identity)

    def one(turn, state):
        return combine(
            state, jax.tree.map(lambda a: lax.dynamic_index_in_dim(a, turn, 0, False), gathered)
        )

    return lax.fori_loop(0, place, one, state)


def mat(left, right):
    return jnp.einsum("...ij,...jk->...ik", left, right, precision=highest)


def mat_t(left, right):
    return jnp.einsum("...ji,...jk->...ik", left, right, precision=highest)


def gram_bt(left, right):
    return jnp.einsum("...ij,...kj->...ik", left, right, preferred_element_type=jnp.float32)


def unit_norm(raw):
    return raw / jnp.sqrt(jnp.sum(raw * raw, -1, keepdims=True) + 1e-06)


def span_terms(gram, keys, values, rates):
    size = keys.shape[-2]
    eye = jnp.eye(size, dtype=keys.dtype)
    lower = jnp.tril(rates[..., :, None] * gram, -1)
    inverse = eye - lower
    power = lower
    for level in range(size.bit_length() - 2):
        power = mat(power, power)
        inverse = mat(inverse, eye + power)
    weights = mat(inverse, rates[..., :, None] * keys)
    updates = mat(inverse, rates[..., :, None] * values)
    return (weights, updates)


def combine_pairs(earlier, later):
    first_m, first_b = earlier
    second_m, second_b = later
    return (mat(second_m, first_m), mat(second_m, first_b) + second_b)


def body(tokens, w_query, w_key, w_value, w_beta, beta_gain, norm_gain, w_out):
    per = w_query.shape[1]
    heads = w_beta.shape[1]
    width = per // heads
    piece = lax.all_gather(tokens, "head", axis=0, tiled=True)
    projected = jnp.concatenate(
        [
            jnp.dot(piece, w_query, preferred_element_type=jnp.float32),
            jnp.dot(piece, w_key, preferred_element_type=jnp.float32),
            jnp.dot(piece, w_value, preferred_element_type=jnp.float32),
            jnp.dot(piece, w_beta, preferred_element_type=jnp.float32),
        ],
        1,
    )
    rows = projected.shape[0]

    def stored(part):
        rounded = part.astype(jnp.bfloat16)
        return lax.optimization_barrier(rounded).astype(jnp.float32).reshape(rows, heads, width)

    query_half = unit_norm(stored(projected[:, :per])).astype(jnp.bfloat16)
    key_half = unit_norm(stored(projected[:, per : 2 * per])).astype(jnp.bfloat16)
    value = stored(projected[:, 2 * per : 3 * per])
    beta = beta_gain[None, :] * jax.nn.sigmoid(projected[:, 3 * per :])
    count = rows // SPAN

    def blocks(array):
        return array.reshape(count, SPAN, heads, width).transpose(0, 2, 1, 3)

    q_half_blocks = blocks(query_half)
    k_half_blocks = blocks(key_half)
    q_blocks = q_half_blocks.astype(jnp.float32)
    k_blocks = k_half_blocks.astype(jnp.float32)
    v_blocks = blocks(value)
    b_blocks = beta.reshape(count, SPAN, heads).transpose(0, 2, 1)
    key_gram = gram_bt(k_half_blocks, k_half_blocks)
    weights, updates = span_terms(key_gram, k_blocks, v_blocks, b_blocks)
    eye_state = jnp.broadcast_to(jnp.eye(width, dtype=jnp.float32), (heads, width, width))
    zero_state = jnp.zeros((heads, width, width), jnp.float32)

    def fold(carry, inputs):
        k_blk, w_blk, u_blk = inputs
        step_pair = (eye_state - mat_t(k_blk, w_blk), mat_t(k_blk, u_blk))
        return (combine_pairs(carry, step_pair), carry)

    (trans_dev, adds_dev), starts = lax.scan(
        fold, (eye_state, zero_state), (k_blocks, weights, updates), unroll=2
    )
    prefix = entering((trans_dev, adds_dev), "seq", combine_pairs, (eye_state, zero_state))
    incoming = prefix[1]
    causal = jnp.tril(jnp.ones((SPAN, SPAN), jnp.float32))

    def emit(state, inputs):
        q_blk, q_half, k_half, k_blk, w_blk, u_blk = inputs
        fresh = u_blk - mat(w_blk, state)
        out = mat(q_blk, state) + mat(causal * gram_bt(q_half, k_half), fresh)
        return (state + mat_t(k_blk, fresh), out)

    final, outs = lax.scan(
        emit,
        incoming,
        (q_blocks, q_half_blocks, k_half_blocks, k_blocks, weights, updates),
        unroll=2,
    )
    heads_out = outs.transpose(0, 2, 1, 3).reshape(rows, heads, width)
    scaled = heads_out / jnp.sqrt(jnp.mean(heads_out * heads_out, -1, keepdims=True) + 1e-05)
    normed = (scaled * norm_gain.reshape(heads, width)).reshape(rows, per).astype(jnp.bfloat16)
    piece = normed
    mixed = lax.psum_scatter(
        jnp.dot(piece, w_out, preferred_element_type=jnp.float32),
        "head",
        scatter_dimension=0,
        tiled=True,
    )
    return mixed.astype(jnp.bfloat16)


def solution(mesh):
    placed = (
        P(("seq", "head"), None),
        P(None, "head"),
        P(None, "head"),
        P(None, "head"),
        P(None, "head"),
        P("head"),
        P("head"),
        P("head", None),
    )
    return jax.shard_map(
        body, mesh=mesh, in_specs=placed, out_specs=P(("seq", "head"), None), check_vma=False
    )
```

profile of v0, /device:TPU:0, one launch (start us, length us, event | category | flops | bytes accessed | tf_op | source)
XLA Modules:
  0.0 978.2 jit_solution(10635402580201143054)
XLA Ops:
  7.4 153.9 %all-gather.6.cloned.1.call-done = bf16[2048,2048]{1,0:T(8,128)(2,1)} async-done(((bf16[512,2048]{1,0:T(8,128)(2,1)}), bf16[2048,2048]{1,0:T(8,128)(2,1)}) %all-gather.6.cloned.1.call-update) | async-done | bytes 8388624 | tf_op jit(solution)/shard_map/all_gather | solution.py:63
  161.3 8.5 convolution_convert_fusion.2
  171.1 2.6 convert_multiply_fusion.1
  173.7 5.0 reshape.139
  178.7 5.7 fusion.51
  184.5 9.8 %convolution_convert_fusion.1 = bf16[2048,512]{1,0:T(8,128)(2,1)} fusion(bf16[2048,2048]{1,0:T(8,128)(2,1)} %all-gather.6.cloned.1.call-done, bf16[2048,512]{1,0:T(8,128)(2,1)} %param.17), kind=kOutput, calls=%fused_computation.86 | convolution fusion | flops 4296015872 | bytes 12582912 | tf_op jit(solution)/shard_map/dot_general | solution.py:68
  194.3 4.8 reshape.150
  199.1 5.3 mul.72
  204.3 6.0 reduce_sum.27
  210.3 2.5 add_sqrt_fusion.1
  212.8 1.6 copy.31
  214.4 6.5 bitcast_convert_fusion
  222.2 5.3 fusion.47
  227.5 4.7 fusion.81
  232.2 5.4 fusion.44
  237.6 5.4 fusion.82
  243.0 5.0 fusion.42
  248.0 4.8 fusion.83
  252.8 5.2 fusion.40
  258.0 4.7 fusion.84
  262.7 5.4 fusion.38
  268.1 5.0 fusion.36
  273.1 5.9 fusion.34
  279.0 5.8 fusion.31
  284.8 127.1 %while.42 = (s32[]{:T(128)}, f32[4,128,128]{2,1,0:T(8,128)S(1)}, f32[4,128,128]{2,1,0:T(8,128)S(1)}, f32[16,2,4,64,128]{4,3,2,1,0:T(8,128)}, f32[16,2,4,64,128]{...) while((s32[]{:T(128)}, f32[4,128,128]{2,1,0:T(8,128)S(1)}, ...), condition=%wide.region_2.3_spmd.clone.clone, body=%wide.region_1.0_spmd.clone.clone.sunk | while | flops 604307456 | bytes 5904515 | solution.py:104
  285.0 1.6 convolution_subtract_fusion.10
  291.3 1.6 convolution_add_fusion.16
  292.9 1.6 convolution_subtract_fusion.10
  299.3 1.6 convolution_add_fusion.16
  300.9 1.6 convolution_subtract_fusion.10
  307.2 1.6 convolution_add_fusion.16
  308.8 1.6 convolution_subtract_fusion.10
  315.1 1.6 convolution_add_fusion.16
  323.1 1.6 convolution_add_fusion.16
  324.7 1.6 convolution_subtract_fusion.10
  331.0 1.6 convolution_add_fusion.16
  338.9 1.6 convolution_add_fusion.16
  340.5 1.6 convolution_subtract_fusion.10
  346.9 1.6 convolution_add_fusion.16
  348.5 1.6 convolution_subtract_fusion.10
  354.8 1.6 convolution_add_fusion.16
  362.7 1.6 convolution_add_fusion.16
  364.3 1.6 convolution_subtract_fusion.10
  370.7 1.6 convolution_add_fusion.16
  378.6 1.6 convolution_add_fusion.16
  386.5 1.6 convolution_add_fusion.16
  394.5 1.6 convolution_add_fusion.16
  402.4 1.6 convolution_add_fusion.16
  410.3 1.6 convolution_add_fusion.16
  413.4 9.8 %convolution_convert_fusion = bf16[2048,512]{1,0:T(8,128)(2,1)} fusion(bf16[2048,2048]{1,0:T(8,128)(2,1)} %all-gather.6.cloned.1.call-done, bf16[2048,512]{1,0:T(8,128)(2,1)} %param.15), kind=kOutput, calls=%fused_computation.85 | convolution fusion | flops 4296015872 | bytes 12582912 | tf_op jit(solution)/shard_map/dot_general | solution.py:66
  423.3 4.8 reshape.144
  428.0 4.2 convert_multiply_fusion
  432.2 5.3 mul.81
  437.5 5.1 reduce_sum.28
  442.8 4.4 fusion.68
  449.1 2.4 reshape.146
  451.6 17.2 %all-gather.8.cloned.1.call-done = f32[32,128,128]{2,1,0:T(8,128)} async-done(((f32[4,128,128]{2,1,0:T(8,128)}), f32[32,128,128]{2,1,0:T(8,128)}) %all-gather.8.cloned.1.call-update) | async-done | bytes 2097168 | tf_op jit(solution)/shard_map/all_gather | solution.py:12
  469.0 185.6 %while.41 = (s32[]{:T(128)}, f32[4,128,128]{2,1,0:T(8,128)S(1)}, f32[16,2,4,64,128]{4,3,2,1,0:T(8,128)}, f32[16,2,4,64,128]{4,3,2,1,0:T(8,128)}, f32[16,2,4,64,1...) while((s32[]{:T(128)}, f32[4,128,128]{2,1,0:T(8,128)S(1)}, ...), condition=%wide.region_7.8_spmd.clone.clone, body=%wide.region_6.7_spmd.clone.clone.sunk | while | flops 361078784 | bytes 5822629 | solution.py:117
  654.7 5.2 fusion.30
  659.9 3.6 copy.39
  663.9 4.7 div.45
  668.6 8.1 fusion.52
  676.7 290.7 %reduce-scatter.2.cloned.1.call-done = f32[512,2048]{1,0:T(8,128)} async-done(((f32[2048,2048]{1,0:T(8,128)}), f32[512,2048]{1,0:T(8,128)}) %reduce-scatter.2.cloned.1.call-update) | async-done | bytes 4194320 | tf_op jit(solution)/shard_map/reduce_scatter | solution.py:127
  967.4 3.8 convert_element_type.69
  (342 shorter events, 279.9 us)
Async XLA Ops:
  6.5 662.0 %copy-start = (bf16[512,2048]{1,0:T(8,128)(2,1)S(1)}, bf16[512,2048]{1,0:T(8,128)(2,1)}, u32[]{:S(2)}) copy-start(bf16[512,2048]{1,0:T(8,128)(2,1)} %param.21) | copy-start | bytes 6291460
  6.5 154.8 %all-gather.6.cloned.1.call-start = ((), (), s32[]{:S(2)}) async-start(), calls=%async_computation.1 | async-start | bytes 10485760 | tf_op jit(solution)/shard_map/all_gather | solution.py:63
  7.3 444.3 %all-gather.10.cloned.1.call-start = ((), (), s32[]{:S(2)}) async-start(), calls=%async_computation.4 | async-start | bytes 2359296 | tf_op jit(solution)/shard_map/all_gather | solution.py:12
  169.8 1.3 copy-start.7
  173.7 5.0 copy-start.8
  173.7 5.0 copy-start.9
  220.9 52.1 %copy-start.1 = (bf16[32,64,4,128]{3,1,2,0:T(8,128)(2,1)}, bf16[32,64,4,128]{3,1,2,0:T(8,128)(2,1)S(1)}, u32[]{:S(2)}) copy-start(bf16[32,64,4,128]{3,1,2,0:T(8,128)(2,1)S(1)} %get-tuple-element.281) | copy-start | bytes 6291460
  273.1 5.9 copy-start.2
  411.9 0.7 copy-start.6
  411.9 0.8 copy-start.4
  412.6 56.1 %all-gather.8.cloned.1.call-start = ((), (), s32[]{:S(2)}) async-start(), calls=%async_computation.3 | async-start | bytes 2359296 | tf_op jit(solution)/shard_map/all_gather | solution.py:12
  413.4 554.1 %reduce-scatter.2.cloned.1.call-start = ((), (), s32[]{:S(2)}) async-start(), calls=%async_computation.2 | async-start | bytes 20971520 | tf_op jit(solution)/shard_map/reduce_scatter | solution.py:127
  447.8 1.3 copy-start.5
  654.7 5.2 copy-start.3
  663.5 5.0 copy-start.10
Sparse Core Ops, SparseCore 0:
  8.9 152.3 all-gather.5
  412.8 26.1 all-gather.9
  440.8 27.8 all-gather.7
  676.8 290.5 reduce-scatter.1
where the time goes:
time: 987 us; the launch traced here: 978 us
  waiting for transfers between devices  463 us (47%)
  matrix products  404 us (41%)
  other arithmetic  55.2 us (6%)
  local copies, waits for them, and re-layouts  39 us (4%)
  between operations  13.9 us (1%)
    reduce_scatter x1, waiting for transfers between devices, body(): lax.psum_scatter(jnp.dot(piece, w_out, preferred_element_type=jnp.float32...  291 us
    dot_general x172, matrix products, mat(): return jnp.einsum('...ij,...jk->...ik', left, right, precision=highest)  179 us
    all_gather x1, waiting for transfers between devices, body(): piece = lax.all_gather(tokens, 'head', axis=0, tiled=True)  154 us
    dot_general x96, matrix products, mat_t(): return jnp.einsum('...ji,...jk->...ik', left, right, precision=highest)  149 us
    dot_general x33, matrix products, gram_bt(): jnp.einsum('...ij,...kj->...ik', left, right, preferred_element_type=jnp....  33.9 us
  transfers between devices with their start and end apart: 4, of which 3 were waited for; matrix products, arithmetic and copies ran while one was open for 4% of the time, Pallas kernels for 0%

commit v1 on v0

--- a/solution.py
+++ b/solution.py
@@ -60,7 +60,15 @@
     per = w_query.shape[1]
     heads = w_beta.shape[1]
     width = per // heads
-    piece = lax.all_gather(tokens, "head", axis=0, tiled=True)
+    ways, here, step = (lax.axis_size("head"), lax.axis_index("head"), tokens.shape[0])
+    line, have = (tokens, 1)
+    while have < ways:
+        line = jnp.concatenate(
+            [line, lax.ppermute(line, "head", [(d, (d - have) % ways) for d in range(ways)])],
+            axis=0,
+        )
+        have = 2 * have
+    piece = jnp.roll(line, here * step, axis=0)
     projected = jnp.concatenate(
         [
             jnp.dot(piece, w_query, preferred_element_type=jnp.float32),

time: 987 us -> 1090 us (1.10)
  waiting for transfers between devices: 463 us -> 534 us
    ppermute x0 -> x2, waiting for transfers between devices: none -> 224 us  [body(): lax.ppermute(line, 'head', [(d, (d - have) % ways) for d in range(ways)])]
    all_gather x1 -> x0, waiting for transfers between devices: 154 us -> none  [body(): piece = lax.all_gather(tokens, 'head', axis=0, tiled=True)]
  transfers between devices with their start and end apart: 4 -> 5, of which waited for: 3 -> 4; matrix products, arithmetic and copies ran while one was open for 4% -> 4% of each run, Pallas kernels for 0% -> 0%
where the time goes in v1:
time: 1090 us; the launch traced here: 1080 us
  waiting for transfers between devices  534 us (49%)
  matrix products  409 us (38%)
  other arithmetic  59.7 us (5%)
  local copies, waits for them, and re-layouts  49.4 us (5%)
  between operations  13.9 us (1%)
    reduce_scatter x1, waiting for transfers between devices, body(): lax.psum_scatter(jnp.dot(piece, w_out, preferred_element_type=jnp.float32...  291 us
    ppermute x2, waiting for transfers between devices, body(): lax.ppermute(line, 'head', [(d, (d - have) % ways) for d in range(ways)])  224 us
    dot_general x172, matrix products, mat(): return jnp.einsum('...ij,...jk->...ik', left, right, precision=highest)  187 us
    dot_general x96, matrix products, mat_t(): return jnp.einsum('...ji,...jk->...ik', left, right, precision=highest)  149 us
    dot_general x33, matrix products, gram_bt(): jnp.einsum('...ij,...kj->...ik', left, right, preferred_element_type=jnp....  35.8 us
  transfers between devices with their start and end apart: 5, of which 4 were waited for; matrix products, arithmetic and copies ran while one was open for 4% of the time, Pallas kernels for 0%

profile of v1, /device:TPU:0, one launch (start us, length us, event | category | flops | bytes accessed | tf_op | source)
XLA Modules:
  0.0 1076.3 jit_solution(7593645152501770436)
XLA Ops:
  6.5 5.0 collective-permute-start
  11.6 45.2 %collective-permute-done = bf16[512,2048]{1,0:T(8,128)(2,1)S(1)} collective-permute-done((bf16[512,2048]{1,0:T(8,128)(2,1)}, bf16[512,2048]{1,0:T(8,128)(2,1)S(1)}, u32[]{:S(2)}, u32[]{:S(2)}) %collective-permute-start) | collective-permute-done | bytes 2097184 | tf_op jit(solution)/shard_map/ppermute | solution.py:67
  56.8 4.9 pad_maximum_fusion
  63.1 1.9 constant_dynamic-update-slice_fusion.5
  65.5 178.7 %collective-permute-done.1 = bf16[1024,2048]{1,0:T(8,128)(2,1)} collective-permute-done((bf16[1024,2048]{1,0:T(8,128)(2,1)}, bf16[1024,2048]{1,0:T(8,128)(2,1)}, u32[]{:S(2)}, u32[]{:S(2)}) %collective-permute-start.1) | collective-permute-done | bytes 4194336 | tf_op jit(solution)/shard_map/ppermute | solution.py:67
  244.2 2.5 constant_dynamic-update-slice_fusion.3
  247.2 2.6 constant_dynamic-update-slice_fusion
  250.1 4.7 fusion.56
  257.1 2.5 convert_multiply_fusion.1
  259.6 4.8 reshape.139
  264.5 5.3 mul.76
  269.7 6.0 reduce_sum.27
  275.7 2.5 add_sqrt_fusion.1
  278.2 1.6 copy.31
  279.8 6.1 bitcast_convert_fusion
  287.3 3.2 fusion.82
  290.5 5.7 fusion.77
  296.3 8.8 fusion.55
  305.1 4.7 fusion.113
  309.9 5.2 fusion.52
  315.1 5.6 fusion.114
  320.6 4.8 fusion.50
  325.4 5.7 fusion.115
  331.1 4.8 fusion.48
  335.9 4.8 fusion.116
  340.7 5.2 fusion.46
  345.9 5.4 fusion.44
  351.4 6.0 fusion.42
  357.3 9.3 fusion.59
  366.7 4.8 reshape.150
  371.5 9.9 fusion.39
  381.4 127.0 %while.42 = (s32[]{:T(128)}, f32[4,128,128]{2,1,0:T(8,128)S(1)}, f32[4,128,128]{2,1,0:T(8,128)S(1)}, f32[16,2,4,64,128]{4,3,2,1,0:T(8,128)}, f32[16,2,4,64,128]{...) while((s32[]{:T(128)}, f32[4,128,128]{2,1,0:T(8,128)S(1)}, ...), condition=%wide.region_2.3_spmd.clone.clone, body=%wide.region_1.2_spmd.clone.clone.sunk | while | flops 604307456 | bytes 5904515 | solution.py:112
  387.7 1.6 convolution_add_fusion.16
  395.6 1.6 convolution_add_fusion.16
  398.8 1.6 convolution_subtract_fusion.11
  403.6 1.6 convolution_add_fusion.16
  411.5 1.6 convolution_add_fusion.16
  419.5 1.6 convolution_add_fusion.16
  427.4 1.6 convolution_add_fusion.16
  435.3 1.6 convolution_add_fusion.16
  443.3 1.6 convolution_add_fusion.16
  451.2 1.6 convolution_add_fusion.16
  459.1 1.6 convolution_add_fusion.16
  467.1 1.6 convolution_add_fusion.16
  475.0 1.6 convolution_add_fusion.16
  483.0 1.6 convolution_add_fusion.16
  490.9 1.6 convolution_add_fusion.16
  498.8 1.6 convolution_add_fusion.16
  506.8 1.6 convolution_add_fusion.16
  510.1 9.8 fusion.62
  519.9 4.7 reshape.144
  524.7 4.2 convert_multiply_fusion
  528.9 5.3 mul.85
  534.1 5.1 reduce_sum.28
  539.5 4.4 fusion.96
  545.8 2.4 reshape.146
  548.2 18.7 %all-gather.7.cloned.1.call-done = f32[32,128,128]{2,1,0:T(8,128)} async-done(((f32[4,128,128]{2,1,0:T(8,128)}), f32[32,128,128]{2,1,0:T(8,128)}) %all-gather.7.cloned.1.call-update) | async-done | bytes 2097168 | tf_op jit(solution)/shard_map/all_gather | solution.py:12
  567.2 185.5 %while.41 = (s32[]{:T(128)}, f32[4,128,128]{2,1,0:T(8,128)S(1)}, f32[16,2,4,64,128]{4,3,2,1,0:T(8,128)}, f32[16,2,4,64,128]{4,3,2,1,0:T(8,128)}, f32[16,2,4,64,1...) while((s32[]{:T(128)}, f32[4,128,128]{2,1,0:T(8,128)S(1)}, ...), condition=%wide.region_7.8_spmd.clone.clone, body=%wide.region_6.7_spmd.clone.clone.sunk | while | flops 361078784 | bytes 5822629 | solution.py:125
  752.7 5.2 fusion.38
  758.0 3.6 copy.39
  761.9 4.7 div.45
  766.6 8.1 fusion.80
  774.8 290.7 %reduce-scatter.2.cloned.1.call-done = f32[512,2048]{1,0:T(8,128)} async-done(((f32[2048,2048]{1,0:T(8,128)}), f32[512,2048]{1,0:T(8,128)}) %reduce-scatter.2.cloned.1.call-update) | async-done | bytes 4194320 | tf_op jit(solution)/shard_map/reduce_scatter | solution.py:135
  1065.5 3.8 convert_element_type.69
  (365 shorter events, 294.0 us)
Async XLA Ops:
  6.5 760.1 %copy-start = (bf16[512,2048]{1,0:T(8,128)(2,1)S(1)}, bf16[512,2048]{1,0:T(8,128)(2,1)}, u32[]{:S(2)}) copy-start(bf16[512,2048]{1,0:T(8,128)(2,1)} %param.21) | copy-start | bytes 6291460
  6.5 541.7 %all-gather.5.cloned.1.call-start = ((), (), s32[]{:S(2)}) async-start(), calls=%async_computation.2 | async-start | bytes 2359296 | tf_op jit(solution)/shard_map/all_gather | solution.py:12
  6.5 50.3 %collective-permute-start = (bf16[512,2048]{1,0:T(8,128)(2,1)}, bf16[512,2048]{1,0:T(8,128)(2,1)S(1)}, u32[]{:S(2)}, u32[]{:S(2)}) collective-permute-start(bf16[512,2048]{1,0:T(8,128)(2,1)} %param.14), channel_id=1, source_target_pairs={{0,3},{1,0},{2,1},{3,2},{4,7},{5,4},{6,5},{7,6},{8,11},{9,8},{10,9... | collective-permute-start | bytes 6291464 | tf_op jit(solution)/shard_map/ppermute | solution.py:67
  56.8 4.9 copy-start.6
  61.7 182.5 %collective-permute-start.1 = (bf16[1024,2048]{1,0:T(8,128)(2,1)}, bf16[1024,2048]{1,0:T(8,128)(2,1)}, u32[]{:S(2)}, u32[]{:S(2)}) collective-permute-start(bf16[1024,2048]{1,0:T(8,128)(2,1)} %pad_maximum_fusion), channel_id=1, source_target_pairs={{0,2},{1,3},{2,0},{3,1},{4,6},{5,7},{6,4},{7,5},{8,10},{9,11},{10,... | collective-permute-start | bytes 12582920 | tf_op jit(solution)/shard_map/ppermute | solution.py:67
  63.0 2.2 copy-start.7
  65.5 181.2 %copy-start.5 = (bf16[512,2048]{1,0:T(8,128)(2,1)S(1)}, bf16[512,2048]{1,0:T(8,128)(2,1)}, u32[]{:S(2)}) copy-start(bf16[512,2048]{1,0:T(8,128)(2,1)} %param.14) | copy-start | bytes 6291460
  247.2 2.9 copy-start.16
  250.1 5.7 copy-start.13
  255.8 1.3 copy-start.12
  285.9 1.3 copy-start.3
  285.9 4.5 copy-start.14
  285.9 4.5 copy-start.15
  305.1 4.7 copy-start.2
  345.9 5.4 copy-start.4
  351.4 6.0 copy-start.1
  351.4 6.0 copy-start.17
  508.4 0.7 copy-start.9
  508.4 0.8 copy-start.11
  509.1 57.9 %all-gather.7.cloned.1.call-start = ((), (), s32[]{:S(2)}) async-start(), calls=%async_computation.3 | async-start | bytes 2359296 | tf_op jit(solution)/shard_map/all_gather | solution.py:12
  509.8 555.6 %reduce-scatter.2.cloned.1.call-start = ((), (), s32[]{:S(2)}) async-start(), calls=%async_computation.1 | async-start | bytes 20971520 | tf_op jit(solution)/shard_map/reduce_scatter | solution.py:135
  544.5 1.3 copy-start.10
  752.7 5.2 copy-start.8
  761.6 5.0 copy-start.18
Sparse Core Ops, SparseCore 0:
  509.2 27.8 all-gather.4
  539.0 27.8 all-gather.6
  774.9 290.5 reduce-scatter.1
